TPU v7x, 128 devices: a whole 4x4x4 slice. The times are simulated.
128 devices in a mesh: grp: 8 (over z, core), dev: 16 (over x, y).
Axes of the slice: x: 4, y: 4, z: 4, core: 2. Of those that a mesh axis runs over, the one named last changes fastest.
Arguments:
- velocity_old: float32 [512, 3, 32, 1024], P(('grp', 'dev')), may hold values from -6 to 6
- viscosity_old: float32 [512, 32, 1024], P(('grp', 'dev')), may hold values from 0.25 to 4
- source: int32 [512], replicated, may hold values from 0 to 511, as said below
Outputs:
- velocity_new: float32 [512, 3, 32, 1024], P(('grp', 'dev'))
Inputs may be any that keep to these rules, and one draw needn't show every extreme that they name: `source`: A permutation; the old block of new block b lies in the same agglomeration group and has the same place among its device's 4 blocks; the 4 blocks of a new device come from 4 different old devices of its group, and each old device sends 1 block to each of 4 different new devices.
All inputs are finite; a program needn't handle non-finite values.
Results may differ from a plain program's by a relative error of at most 0.0001.
Values sent between devices are 32-bit elements; how exact they have to be, the bound alone decides.
A program may use at most 256 MiB of HBM per device.

v0:
```python
import math
import jax
import jax.numpy as jnp
from jax import lax
from jax.sharding import PartitionSpec as P

SWEEPS = 2
BOTTOM = 8
RELAX_WEIGHT = 0.8
DIFFUSION_NUMBER = 1000.0


def padded_2(cells, sides, width):
    for axis, dim in sides:
        count = lax.axis_size(axis)
        ends = count - 1
        head = lax.slice_in_dim(cells, 0, width, axis=dim)
        tail = lax.slice_in_dim(cells, cells.shape[dim] - width, cells.shape[dim], axis=dim)
        cells = jnp.concatenate(
            [
                lax.ppermute(tail, axis, [(i, (i + 1) % count) for i in range(ends)]),
                cells,
                lax.ppermute(head, axis, [((i + 1) % count, i) for i in range(ends)]),
            ],
            axis=dim,
        )
    return cells


def blocks_to_grid(blocks):
    num_blocks, channels, edge_len = (blocks.shape[0], blocks.shape[1], blocks.shape[2])
    columns = num_blocks // 4
    parted = blocks.reshape(columns, 2, 2, channels, edge_len, edge_len, edge_len)
    parted = parted.transpose(3, 0, 6, 1, 4, 2, 5)
    return parted.reshape(channels, columns * edge_len, 4 * edge_len * edge_len)


def grid_to_blocks(grid):
    channels, length, plane = grid.shape
    edge_len = math.isqrt(plane) // 2
    columns = length // edge_len
    parted = grid.reshape(channels, columns, edge_len, 2, edge_len, 2, edge_len)
    parted = parted.transpose(1, 3, 5, 0, 4, 6, 2)
    return parted.reshape(columns * 4, channels, edge_len, edge_len * edge_len)


def flat_neighbors(array):
    plane = array.shape[2]
    width_y = math.isqrt(plane)
    middle = array[:, 1:-1]
    padded = jnp.pad(middle, ((0, 0), (0, 0), (width_y, width_y)))
    column = jnp.arange(plane) % width_y
    lower_y = jnp.where(column == 0, 0.0, padded[:, :, width_y - 1 : width_y - 1 + plane])
    upper_y = jnp.where(column == width_y - 1, 0.0, padded[:, :, width_y + 1 : width_y + 1 + plane])
    return (
        middle,
        (
            array[:, :-2],
            array[:, 2:],
            padded[:, :, 0:plane],
            padded[:, :, 2 * width_y : 2 * width_y + plane],
            lower_y,
            upper_y,
        ),
    )


def coefficients(viscous, level_coef, pad_along):
    middle, beside_all = flat_neighbors(pad_along(viscous))
    face_coef = tuple((0.5 * (middle + neighbor) for neighbor in beside_all))
    summed = face_coef[0] + face_coef[1] + face_coef[2] + face_coef[3] + face_coef[4] + face_coef[5]
    diagonal = 1.0 + level_coef * summed
    return (face_coef, diagonal)


def operate(solution, face_coef, diagonal, level_coef, pad_along):
    middle, beside_all = flat_neighbors(pad_along(solution))
    summed = face_coef[0] * beside_all[0]
    for index_no in range(1, 6):
        summed = summed + face_coef[index_no] * beside_all[index_no]
    return diagonal * solution - level_coef * summed


def smooth(solution, right_side, face_coef, diagonal, level_coef, pad_along, repeats):
    for sweep_no in range(repeats):
        solution = (
            solution
            + RELAX_WEIGHT
            * (right_side - operate(solution, face_coef, diagonal, level_coef, pad_along))
            / diagonal
        )
    return solution


def coarsen(grid):
    channels, length, plane = grid.shape
    width_y = math.isqrt(plane)
    shaped = grid.reshape(channels, length // 2, 2, width_y // 2, 2, width_y // 2, 2)
    return shaped.mean(axis=(2, 4, 6)).reshape(channels, length // 2, plane // 4)


def refine(grid):
    channels, length, plane = grid.shape
    width_y = math.isqrt(plane)
    shaped = grid.reshape(channels, length, 1, width_y, 1, width_y, 1)
    shaped = jnp.broadcast_to(shaped, (channels, length, 2, width_y, 2, width_y, 2))
    return shaped.reshape(channels, 2 * length, 4 * plane)


def cell_pad(array):
    return padded_2(array, ((("grp", "dev"), 1),), 1)


def group_pad(array):
    return padded_2(array, (("grp", 1),), 1)


def group_bottom(level_rhs, viscous):
    stacked = jnp.concatenate([level_rhs, viscous], axis=0)
    gathered = lax.all_gather(stacked, "dev", axis=1, tiled=True)
    group_rhs = gathered[:3]
    group_visc = gathered[3:]
    level_coef = DIFFUSION_NUMBER / 64.0
    face_coef, diagonal = coefficients(group_visc, level_coef, group_pad)
    solved = smooth(
        jnp.zeros_like(group_rhs), group_rhs, face_coef, diagonal, level_coef, group_pad, BOTTOM
    )
    own_width = level_rhs.shape[1]
    return lax.dynamic_slice_in_dim(solved, lax.axis_index("dev") * own_width, own_width, 1)


def vcycle_solve(right_side, viscous):
    stored = []
    solution = right_side
    level_rhs = right_side
    for level_no in range(3):
        level_coef = DIFFUSION_NUMBER / 4.0**level_no
        face_coef, diagonal = coefficients(viscous, level_coef, cell_pad)
        solution = smooth(solution, level_rhs, face_coef, diagonal, level_coef, cell_pad, SWEEPS)
        residue = level_rhs - operate(solution, face_coef, diagonal, level_coef, cell_pad)
        stored.append((solution, level_rhs, face_coef, diagonal, level_coef))
        level_rhs = coarsen(residue)
        viscous = coarsen(viscous)
        solution = jnp.zeros_like(level_rhs)
    solution = group_bottom(level_rhs, viscous)
    for level_no in (2, 1, 0):
        before, level_rhs, face_coef, diagonal, level_coef = stored[level_no]
        solution = smooth(
            before + refine(solution), level_rhs, face_coef, diagonal, level_coef, cell_pad, SWEEPS
        )
    return solution


def local(velocity_old, viscosity_old, source):
    group_index = lax.axis_index("grp")
    member_index = lax.axis_index("dev")
    member_count = lax.axis_size("dev")
    blk_per = velocity_old.shape[0]
    group_base = group_index * member_count * blk_per
    src_table = (
        lax.dynamic_slice_in_dim(source, group_base, member_count * blk_per).reshape(
            member_count, blk_per
        )
        - group_base
    )
    from_dev = src_table // blk_per
    from_slot = src_table % blk_per
    mine_dev = lax.dynamic_index_in_dim(from_dev, member_index, 0, keepdims=False)
    mine_slot = lax.dynamic_index_in_dim(from_slot, member_index, 0, keepdims=False)
    wanted = mine_dev * blk_per + mine_slot
    pieces = (
        lax.all_gather(velocity_old, "dev", axis=0, tiled=True),
        lax.all_gather(viscosity_old, "dev", axis=0, tiled=True),
    )
    piece_rows = pieces[0].shape[0]
    inside = (wanted >= 0) & (wanted < piece_rows)
    clipped = jnp.clip(wanted, 0, piece_rows - 1)
    new_vel = jnp.where(
        inside[:, None, None, None],
        jnp.take(pieces[0], clipped, axis=0),
        jnp.zeros_like(velocity_old),
    )
    new_visc = jnp.where(
        inside[:, None, None], jnp.take(pieces[1], clipped, axis=0), jnp.zeros_like(viscosity_old)
    )
    right_side = blocks_to_grid(new_vel)
    viscous = blocks_to_grid(new_visc[:, None])
    solution = vcycle_solve(right_side, viscous)
    return grid_to_blocks(solution)


def solution(mesh):
    return jax.shard_map(
        local,
        mesh=mesh,
        in_specs=(P(("grp", "dev"), None, None, None), P(("grp", "dev"), None, None), P()),
        out_specs=P(("grp", "dev"), None, None, None),
        check_vma=False,
    )
```

profile of v0, /device:TPU:31, one launch (start us, length us, event | category | flops | bytes accessed | tf_op | source)
XLA Modules:
  0.0 1013.4 jit_solution(10775965139218544529)
XLA Ops:
  11.0 7.4 collective-permute-start.18
  22.6 57.7 %all-gather.5.cloned.1.call-done = f32[64,32,1024]{2,1,0:T(8,128)} async-done(((f32[4,32,1024]{2,1,0:T(8,128)}), f32[64,32,1024]{2,1,0:T(8,128)}) %all-gather.5.cloned.1.call-update) | async-done | bytes 8388624 | tf_op jit(solution)/shard_map/all_gather | solution.py:173
  86.7 22.0 %reshape_reshape.2 = f32[16,2,32,2,32,2]{1,0,5,4,3,2:T(8,128)} reshape(f32[1,1,32,2,32,2,32]{2,6,5,4,3,1,0:T(8,128)} %fusion.454) | data formatting | bytes 1048576 | tf_op jit(solution)/shard_map/reshape;reshape | solution.py:98
  108.7 12.5 %reduce_sum.55 = f32[16,32,32]{0,2,1:T(8,128)S(1)} reduce(f32[16,2,32,2,32,2]{1,0,5,4,3,2:T(8,128)} %reshape_reshape.2, f32[]{:T(128)} %constant.250.clone.1), dimensions={1,3,5}, to_apply=%region_1.2 | reduce | flops 114688 | bytes 589828 | tf_op jit(solution)/shard_map/reduce_sum | solution.py:99
  140.5 96.1 %all-gather.3.cloned.1.call-done = f32[64,3,32,1024]{3,2,1,0:T(8,128)} async-done(((f32[4,3,32,1024]{3,2,1,0:T(8,128)}), f32[64,3,32,1024]{3,2,1,0:T(8,128)}) %all-gather.3.cloned.1.call-update) | async-done | bytes 25165840 | tf_op jit(solution)/shard_map/all_gather | solution.py:172
  236.7 8.8 gather_fusion
  249.6 10.0 copy.71
  259.5 11.8 %select_bitcast_fusion = f32[3,1,32,2,32,2,32]{6,5,4,3,2,0,1:T(2,128)} fusion(f32[1,2,2,3,32,32,32]{5,2,4,1,6,3,0:T(2,128)} %copy.71, pred[2,2]{1,0:T(4,128)(4,1)S(1)} %compare_and_fusion, pred[2,2]{1,0:T(4,128)(4,1)S(1)} %and.182), kind=kLoop, calls=%fused_computation.2 | loop fusion | flops 786432 | bytes 3145736 | tf_op jit(solution)/shard_map/transpose | solution.py:34
  271.3 9.5 reshape.248
  293.6 7.9 collective-permute-start.8
  305.5 7.9 collective-permute-start.4
  316.1 6.9 collective-permute-done.5
  331.2 6.4 collective-permute-start.10
  342.9 154.0 %reshape.250 = f32[3,16,2,32,2,32,2]{6,5,4,3,2,1,0:T(8,128)} reshape(f32[3,32,4096]{2,1,0:T(8,128)} %fusion.35) | data formatting | bytes 3145728 | tf_op jit(solution)/shard_map/reshape | solution.py:98
  496.9 31.6 %reduce_sum.54 = f32[3,16,32,32]{3,2,1,0:T(8,128)} reduce(f32[3,16,2,32,2,32,2]{6,5,4,3,2,1,0:T(8,128)} %reshape.250, f32[]{:T(128)} %constant.250.clone.1), dimensions={2,4,6}, to_apply=%region_0.1 | reduce | flops 344064 | bytes 1769476 | tf_op jit(solution)/shard_map/reduce_sum | solution.py:99
  537.1 6.4 collective-permute-start.12
  546.8 5.9 collective-permute-done.13
  566.8 14.7 %reshape.251 = f32[3,8,2,16,2,16,2]{6,5,4,3,2,1,0:T(8,128)} reshape(f32[3,16,1024]{2,1,0:T(8,128)} %fusion.106) | data formatting | bytes 393216 | tf_op jit(solution)/shard_map/reshape | solution.py:98
  581.6 6.3 reduce_sum.56
  613.1 6.7 collective-permute-done.23
  624.4 15.4 %all_gather.11 = f32[4,64,64]{2,0,1:T(4,128)S(1)} all-gather(f32[4,4,64]{2,0,1:T(4,128)S(1)} %copy.76), channel_id=1, replica_groups=mesh['grp'=8,'dev'=16] {'dev'}, dimensions={1}, use_global_device_ids=true | all-gather | bytes 69632 | tf_op jit(solution)/shard_map/all_gather | solution.py:120
  639.8 7.6 collective-permute-start.24
  717.9 7.2 collective-permute-done.43
  743.1 10.4 %reshape.254 = f32[3,16,1024]{2,1,0:T(8,128)} reshape(f32[3,8,2,16,2,16,2]{6,5,4,3,2,1,0:T(8,128)} %broadcast_in_dim.360) | data formatting | bytes 393216 | tf_op jit(solution)/shard_map/reshape | solution.py:107
  759.9 5.9 collective-permute-done.47
  781.3 32.2 %broadcast_in_dim.362 = f32[3,16,2,32,2,32,2]{6,5,4,3,2,1,0:T(8,128)} broadcast(f32[3,16,32,32]{3,2,1,0:T(8,128)} %broadcast_in_dim.361), dimensions={0,1,3,5} | broadcast | bytes 1769472 | tf_op jit(solution)/shard_map/broadcast_in_dim | solution.py:106
  813.5 138.7 %reshape.255 = f32[3,32,4096]{2,1,0:T(8,128)} reshape(f32[3,16,2,32,2,32,2]{6,5,4,3,2,1,0:T(8,128)} %broadcast_in_dim.362) | data formatting | bytes 3145728 | tf_op jit(solution)/shard_map/reshape | solution.py:107
  959.8 6.3 collective-permute-done.51
  973.8 6.0 collective-permute-done.53
  982.7 7.7 reshape.256
  990.4 10.1 copy.78
  1000.5 5.9 reshape.257
  (343 shorter events, 254.1 us)
Async XLA Ops:
  6.5 73.8 %all-gather.5.cloned.1.call-start = ((), (), s32[]{:S(2)}) async-start(), calls=%async_computation.1 | async-start | bytes 8912896 | tf_op jit(solution)/shard_map/all_gather | solution.py:173
  7.3 229.4 %all-gather.3.cloned.1.call-start = ((), (), s32[]{:S(2)}) async-start(), calls=%async_computation | async-start | bytes 26738688 | tf_op jit(solution)/shard_map/all_gather | solution.py:172
  8.6 581.9 %collective-permute-start.19 = (f32[3,1,256]{2,1,0:T(1,128)}, f32[3,1,256]{2,1,0:T(1,128)}, u32[]{:S(2)}, u32[]{:S(2)}) collective-permute-start(f32[3,1,256]{2,1,0:T(1,128)} %broadcast.449), channel_id=1, source_target_pairs={{1,0},{2,1},{3,2},{4,3},{5,4},{6,5},{7,6},{8,7},{9,8},{10,9},{11,1... | collective-permute-start | bytes 9224 | tf_op jit(solution)/shard_map/ppermute | solution.py:23
  11.0 579.6 %collective-permute-start.18 = (f32[3,1,256]{2,1,0:T(1,128)}, f32[3,1,256]{2,1,0:T(1,128)}, u32[]{:S(2)}, u32[]{:S(2)}) collective-permute-start(f32[3,1,256]{2,1,0:T(1,128)} %broadcast.449), channel_id=1, source_target_pairs={{0,1},{1,2},{2,3},{3,4},{4,5},{5,6},{6,7},{7,8},{8,9},{9,10},{10,1... | collective-permute-start | bytes 9224 | tf_op jit(solution)/shard_map/ppermute | solution.py:21
  19.0 513.2 %collective-permute-start.11 = (f32[3,1,1024]{2,1,0:T(1,128)}, f32[3,1,1024]{2,1,0:T(1,128)}, u32[]{:S(2)}, u32[]{:S(2)}) collective-permute-start(f32[3,1,1024]{2,1,0:T(1,128)} %broadcast.445), channel_id=1, source_target_pairs={{1,0},{2,1},{3,2},{4,3},{5,4},{6,5},{7,6},{8,7},{9,8},{10,9},{11,1... | collective-permute-start | bytes 36872 | tf_op jit(solution)/shard_map/ppermute | solution.py:23
  129.3 151.6 %collective-permute-start = (f32[1,1,4096]{2,1,0:T(1,128)S(1)}, f32[1,1,4096]{2,1,0:T(1,128)S(1)}, u32[]{:S(2)}, u32[]{:S(2)}) collective-permute-start(f32[1,1,4096]{2,1,0:T(1,128)S(1)} %get-tuple-element.39), channel_id=1, source_target_pairs={{0,1},{1,2},{2,3},{3,4},{4,5},{5,6},{6,7},{7,8},{8,9},{9,10},{10,1... | collective-permute-start | bytes 49160 | tf_op jit(solution)/shard_map/ppermute | solution.py:21
  134.9 151.5 %collective-permute-start.1 = (f32[1,1,4096]{2,1,0:T(1,128)S(1)}, f32[1,1,4096]{2,1,0:T(1,128)S(1)}, u32[]{:S(2)}, u32[]{:S(2)}) collective-permute-start(f32[1,1,4096]{2,1,0:T(1,128)S(1)} %get-tuple-element.40), channel_id=1, source_target_pairs={{1,0},{2,1},{3,2},{4,3},{5,4},{6,5},{7,6},{8,7},{9,8},{10,9},{11,1... | collective-permute-start | bytes 49160 | tf_op jit(solution)/shard_map/ppermute | solution.py:23
  280.9 12.7 %collective-permute-start.2 = (f32[3,1,4096]{2,1,0:T(1,128)S(1)}, f32[3,1,4096]{2,1,0:T(1,128)S(1)}, u32[]{:S(2)}, u32[]{:S(2)}) collective-permute-start(f32[3,1,4096]{2,1,0:T(1,128)S(1)} %get-tuple-element.30), channel_id=1, source_target_pairs={{0,1},{1,2},{2,3},{3,4},{4,5},{5,6},{6,7},{7,8},{8,9},{9,10},{10,1... | collective-permute-start | bytes 147464 | tf_op jit(solution)/shard_map/ppermute | solution.py:21
  286.5 15.0 %collective-permute-start.3 = (f32[3,1,4096]{2,1,0:T(1,128)S(1)}, f32[3,1,4096]{2,1,0:T(1,128)S(1)}, u32[]{:S(2)}, u32[]{:S(2)}) collective-permute-start(f32[3,1,4096]{2,1,0:T(1,128)S(1)} %get-tuple-element.31), channel_id=1, source_target_pairs={{1,0},{2,1},{3,2},{4,3},{5,4},{6,5},{7,6},{8,7},{9,8},{10,9},{11,1... | collective-permute-start | bytes 147464 | tf_op jit(solution)/shard_map/ppermute | solution.py:23
  293.6 11.9 %collective-permute-start.8 = (f32[1,1,1024]{2,1,0:T(1,128)S(1)}, f32[1,1,1024]{2,1,0:T(1,128)S(1)}, u32[]{:S(2)}, u32[]{:S(2)}) collective-permute-start(f32[1,1,1024]{2,1,0:T(1,128)S(1)} %get-tuple-element.73), channel_id=1, source_target_pairs={{0,1},{1,2},{2,3},{3,4},{4,5},{5,6},{6,7},{7,8},{8,9},{9,10},{10,1... | collective-permute-start | bytes 12296 | tf_op jit(solution)/shard_map/ppermute | solution.py:21
  301.5 11.9 %collective-permute-start.9 = (f32[1,1,1024]{2,1,0:T(1,128)S(1)}, f32[1,1,1024]{2,1,0:T(1,128)S(1)}, u32[]{:S(2)}, u32[]{:S(2)}) collective-permute-start(f32[1,1,1024]{2,1,0:T(1,128)S(1)} %get-tuple-element.74), channel_id=1, source_target_pairs={{1,0},{2,1},{3,2},{4,3},{5,4},{6,5},{7,6},{8,7},{9,8},{10,9},{11,1... | collective-permute-start | bytes 12296 | tf_op jit(solution)/shard_map/ppermute | solution.py:23
  305.5 10.6 %collective-permute-start.4 = (f32[3,1,4096]{2,1,0:T(1,128)S(1)}, f32[3,1,4096]{2,1,0:T(1,128)S(1)}, u32[]{:S(2)}, u32[]{:S(2)}) collective-permute-start(f32[3,1,4096]{2,1,0:T(1,128)S(1)} %get-tuple-element.28), channel_id=1, source_target_pairs={{0,1},{1,2},{2,3},{3,4},{4,5},{5,6},{6,7},{7,8},{8,9},{9,10},{10,1... | collective-permute-start | bytes 147464 | tf_op jit(solution)/shard_map/ppermute | solution.py:21
  313.4 9.6 collective-permute-start.5
  327.1 10.6 %collective-permute-start.7 = (f32[3,1,4096]{2,1,0:T(1,128)S(1)}, f32[3,1,4096]{2,1,0:T(1,128)S(1)}, u32[]{:S(2)}, u32[]{:S(2)}) collective-permute-start(f32[3,1,4096]{2,1,0:T(1,128)S(1)} %get-tuple-element.27), channel_id=1, source_target_pairs={{1,0},{2,1},{3,2},{4,3},{5,4},{6,5},{7,6},{8,7},{9,8},{10,9},{11,1... | collective-permute-start | bytes 147464 | tf_op jit(solution)/shard_map/ppermute | solution.py:23
  331.2 204.4 %collective-permute-start.10 = (f32[3,1,1024]{2,1,0:T(1,128)}, f32[3,1,1024]{2,1,0:T(1,128)}, u32[]{:S(2)}, u32[]{:S(2)}) collective-permute-start(f32[3,1,1024]{2,1,0:T(1,128)} %broadcast.445), channel_id=1, source_target_pairs={{0,1},{1,2},{2,3},{3,4},{4,5},{5,6},{6,7},{7,8},{8,9},{9,10},{10,1... | collective-permute-start | bytes 36872 | tf_op jit(solution)/shard_map/ppermute | solution.py:21
  337.7 205.8 %collective-permute-start.16 = (f32[1,1,256]{2,1,0:T(1,128)}, f32[1,1,256]{2,1,0:T(1,128)}, u32[]{:S(2)}, u32[]{:S(2)}) collective-permute-start(f32[1,1,256]{2,1,0:T(1,128)} %get-tuple-element.89), channel_id=1, source_target_pairs={{0,1},{1,2},{2,3},{3,4},{4,5},{5,6},{6,7},{7,8},{8,9},{9,10},{10,1... | collective-permute-start | bytes 3080 | tf_op jit(solution)/shard_map/ppermute | solution.py:21
  532.2 13.2 %collective-permute-start.17 = (f32[1,1,256]{2,1,0:T(1,128)}, f32[1,1,256]{2,1,0:T(1,128)S(1)}, u32[]{:S(2)}, u32[]{:S(2)}) collective-permute-start(f32[1,1,256]{2,1,0:T(1,128)} %get-tuple-element.90), channel_id=1, source_target_pairs={{1,0},{2,1},{3,2},{4,3},{5,4},{6,5},{7,6},{8,7},{9,8},{10,9},{11,1... | collective-permute-start | bytes 3080 | tf_op jit(solution)/shard_map/ppermute | solution.py:23
  537.1 9.8 collective-permute-start.12
  543.5 9.2 collective-permute-start.13
  556.0 9.2 collective-permute-start.15
  591.4 13.6 %collective-permute-start.20 = (f32[3,1,256]{2,1,0:T(1,128)S(1)}, f32[3,1,256]{2,1,0:T(1,128)S(1)}, u32[]{:S(2)}, u32[]{:S(2)}) collective-permute-start(f32[3,1,256]{2,1,0:T(1,128)S(1)} %get-tuple-element.81), channel_id=1, source_target_pairs={{0,1},{1,2},{2,3},{3,4},{4,5},{5,6},{6,7},{7,8},{8,9},{9,10},{10,1... | collective-permute-start | bytes 9224 | tf_op jit(solution)/shard_map/ppermute | solution.py:21
  593.7 11.4 %collective-permute-start.21 = (f32[3,1,256]{2,1,0:T(1,128)S(1)}, f32[3,1,256]{2,1,0:T(1,128)S(1)}, u32[]{:S(2)}, u32[]{:S(2)}) collective-permute-start(f32[3,1,256]{2,1,0:T(1,128)S(1)} %get-tuple-element.82), channel_id=1, source_target_pairs={{1,0},{2,1},{3,2},{4,3},{5,4},{6,5},{7,6},{8,7},{9,8},{10,9},{11,1... | collective-permute-start | bytes 9224 | tf_op jit(solution)/shard_map/ppermute | solution.py:23
  597.3 55.3 %collective-permute-start.27 = (f32[3,1,64]{2,0,1:T(4,128)}, f32[3,1,64]{2,0,1:T(4,128)}, u32[]{:S(2)}, u32[]{:S(2)}) collective-permute-start(f32[3,1,64]{2,0,1:T(4,128)} %broadcast.453), channel_id=1, source_target_pairs={{16,0},{32,16},{48,32},{64,48},{80,64},{96,80},{112,96},{17,1},{33... | collective-permute-start | bytes 2312 | tf_op jit(solution)/shard_map/ppermute | solution.py:23
  599.2 53.4 %collective-permute-start.26 = (f32[3,1,64]{2,0,1:T(4,128)}, f32[3,1,64]{2,0,1:T(4,128)}, u32[]{:S(2)}, u32[]{:S(2)}) collective-permute-start(f32[3,1,64]{2,0,1:T(4,128)} %broadcast.453), channel_id=1, source_target_pairs={{0,16},{16,32},{32,48},{48,64},{64,80},{80,96},{96,112},{1,17},{17... | collective-permute-start | bytes 2312 | tf_op jit(solution)/shard_map/ppermute | solution.py:21
  610.7 9.1 collective-permute-start.23
  639.8 9.6 collective-permute-start.24
  716.0 9.1 collective-permute-start.43
  727.3 9.1 collective-permute-start.45
  756.5 9.2 collective-permute-start.47
  769.0 9.2 collective-permute-start.49
  956.4 9.6 collective-permute-start.51
  970.2 9.6 collective-permute-start.53
  (89 other events, 4192.5 us)
Sparse Core Ops, SparseCore 0:
  9.5 70.7 all-gather.4
  82.5 154.1 all-gather.2
where the time goes:
time: 1020 us; the launch traced here: 1010 us
  local copies, waits for them, and re-layouts  462 us (45%)
  waiting for transfers between devices  236 us (23%)
  starting transfers between devices  169 us (17%)
  other arithmetic  115 us (11%)
  between operations  15.6 us (2%)
  blocking collectives  15.4 us (2%)
    reshape x3, local copies, waits for them, and re-layouts, coarsen(): grid.reshape(channels, length // 2, 2, width_y // 2, 2, width_y // 2, 2)  171 us
    reshape x3, local copies, waits for them, and re-layouts, refine(): return shaped.reshape(channels, 2 * length, 4 * plane)  151 us
    ppermute x27, starting transfers between devices, padded_2(): lax.ppermute(tail, axis, [(i, (i + 1) % count) for i in range(ends)])  99.5 us
    all_gather x1, waiting for transfers between devices, local(): lax.all_gather(velocity_old, 'dev', axis=0, tiled=True)  96.1 us
    ppermute x27, waiting for transfers between devices, padded_2(): lax.ppermute(head, axis, [((i + 1) % count, i) for i in range(ends)])  80.7 us
    ppermute x27, starting transfers between devices, padded_2(): lax.ppermute(head, axis, [((i + 1) % count, i) for i in range(ends)])  69.5 us
    all_gather x1, waiting for transfers between devices, local(): lax.all_gather(viscosity_old, 'dev', axis=0, tiled=True)  57.7 us
    reduce_sum x6, other arithmetic, coarsen(): shaped.mean(axis=(2, 4, 6)).reshape(channels, length // 2, plane // 4)  55.9 us
  transfers between devices with their start and end apart: 56, of which 20 were waited for; matrix products, arithmetic and copies ran while one was open for 34% of the time, Pallas kernels for 0%

commit v1 on v0

--- a/solution.py
+++ b/solution.py
@@ -8,6 +8,12 @@
 BOTTOM = 8
 RELAX_WEIGHT = 0.8
 DIFFUSION_NUMBER = 1000.0
+draw_loops = lambda point: jnp.concatenate(
+    jax.lax.all_to_all(
+        jnp.stack(jax.lax.axis_size("dev") * [point]), axis_name="dev", split_axis=0, concat_axis=0
+    ),
+    axis=0,
+)
 
 
 def padded_2(cells, sides, width):
@@ -168,10 +174,7 @@
     mine_dev = lax.dynamic_index_in_dim(from_dev, member_index, 0, keepdims=False)
     mine_slot = lax.dynamic_index_in_dim(from_slot, member_index, 0, keepdims=False)
     wanted = mine_dev * blk_per + mine_slot
-    pieces = (
-        lax.all_gather(velocity_old, "dev", axis=0, tiled=True),
-        lax.all_gather(viscosity_old, "dev", axis=0, tiled=True),
-    )
+    pieces = (lax.all_gather(velocity_old, "dev", axis=0, tiled=True), draw_loops(viscosity_old))
     piece_rows = pieces[0].shape[0]
     inside = (wanted >= 0) & (wanted < piece_rows)
     clipped = jnp.clip(wanted, 0, piece_rows - 1)

time: 1020 us -> 1060 us (1.039)
  starting transfers between devices: 169 us -> 224 us
  waiting for transfers between devices: 236 us -> 208 us
  local copies, waits for them, and re-layouts: 462 us -> 478 us
    all_to_all x0 -> x1, waiting for transfers between devices: none -> 112 us  [jax.lax.all_to_all(jnp.stack(jax.lax.axis_size('dev') * [point]), axis_na...]
    all_gather x1, waiting for transfers between devices: 96.1 us -> 10.5 us  [local(): lax.all_gather(velocity_old, 'dev', axis=0, tiled=True)]
    all_gather x1 -> x0, waiting for transfers between devices: 57.7 us -> none  [local(): lax.all_gather(viscosity_old, 'dev', axis=0, tiled=True)]
    ppermute x27, starting transfers between devices: 99.5 us -> 148 us  [padded_2(): lax.ppermute(tail, axis, [(i, (i + 1) % count) for i in range(ends)])]
  transfers between devices with their start and end apart: 56 -> 56, of which waited for: 20 -> 21; matrix products, arithmetic and copies ran while one was open for 34% -> 34% of each run, Pallas kernels for 0% -> 0%
where the time goes in v1:
time: 1060 us; the launch traced here: 1050 us
  local copies, waits for them, and re-layouts  478 us (45%)
  starting transfers between devices  224 us (21%)
  waiting for transfers between devices  208 us (20%)
  other arithmetic  113 us (11%)
  between operations  15.6 us (1%)
  blocking collectives  15.4 us (1%)
    reshape x3, local copies, waits for them, and re-layouts, coarsen(): grid.reshape(channels, length // 2, 2, width_y // 2, 2, width_y // 2, 2)  171 us
    reshape x3, local copies, waits for them, and re-layouts, refine(): return shaped.reshape(channels, 2 * length, 4 * plane)  151 us
    ppermute x27, starting transfers between devices, padded_2(): lax.ppermute(tail, axis, [(i, (i + 1) % count) for i in range(ends)])  148 us
    all_to_all x1, waiting for transfers between devices, jax.lax.all_to_all(jnp.stack(jax.lax.axis_size('dev') * [point]), axis_na...  112 us
    ppermute x27, waiting for transfers between devices, padded_2(): lax.ppermute(head, axis, [((i + 1) % count, i) for i in range(ends)])  84.6 us
    ppermute x27, starting transfers between devices, padded_2(): lax.ppermute(head, axis, [((i + 1) % count, i) for i in range(ends)])  68.8 us
    reduce_sum x6, other arithmetic, coarsen(): shaped.mean(axis=(2, 4, 6)).reshape(channels, length // 2, plane // 4)  55.8 us
    broadcast_in_dim x6, local copies, waits for them, and re-layouts, refine(): jnp.broadcast_to(shaped, (channels, length, 2, width_y, 2, width_y, 2))  42.3 us
  transfers between devices with their start and end apart: 56, of which 21 were waited for; matrix products, arithmetic and copies ran while one was open for 34% of the time, Pallas kernels for 0%

profile of v1, /device:TPU:31, one launch (start us, length us, event | category | flops | bytes accessed | tf_op | source)
XLA Modules:
  0.0 1053.7 jit_solution(6212185109947118065)
XLA Ops:
  12.0 6.5 all-to-all-start
  25.9 7.8 collective-permute-start.18
  35.5 111.6 %all-to-all-done = f32[16,4,32,1024]{3,2,1,0:T(8,128)} async-done(((f32[16,4,32,1024]{3,2,1,0:T(8,128)}), f32[16,4,32,1024]{3,2,1,0:T(8,128)}, u32[]{:S(2)}, u32[]{:S(2)}) %all-to-all-start) | async-done | bytes 8388640 | tf_op jit(solution)/shard_map/all_to_all | solution.py:12
  162.5 22.2 %reshape_reshape.2 = f32[16,2,32,2,32,2]{1,0,5,4,3,2:T(8,128)} reshape(f32[1,1,32,2,32,2,32]{2,6,5,4,3,1,0:T(8,128)} %copy.72) | data formatting | bytes 1048576 | tf_op jit(solution)/shard_map/reshape;reshape | solution.py:104
  184.7 12.6 %reduce_sum.55 = f32[16,32,32]{0,2,1:T(8,128)S(1)} reduce(f32[16,2,32,2,32,2]{1,0,5,4,3,2:T(8,128)} %reshape_reshape.2, f32[]{:T(128)} %constant.250.clone.1), dimensions={1,3,5}, to_apply=%region_1.2 | reduce | flops 114688 | bytes 589828 | tf_op jit(solution)/shard_map/reduce_sum | solution.py:105
  205.8 45.1 %collective-permute-start = (f32[1,1,4096]{2,1,0:T(1,128)S(1)}, f32[1,1,4096]{2,1,0:T(1,128)S(1)}, u32[]{:S(2)}, u32[]{:S(2)}) collective-permute-start(f32[1,1,4096]{2,1,0:T(1,128)S(1)} %get-tuple-element.39), channel_id=1, source_target_pairs={{0,1},{1,2},{2,3},{3,4},{4,5},{5,6},{6,7},{7,8},{8,9},{9,10},{10,1... | collective-permute-start | bytes 49160 | tf_op jit(solution)/shard_map/ppermute | solution.py:27
  256.3 10.5 all-gather.2.cloned.1.call-done
  266.8 8.8 gather_fusion
  279.7 10.0 copy.70
  289.7 11.8 %select_bitcast_fusion = f32[3,1,32,2,32,2,32]{6,5,4,3,2,0,1:T(2,128)} fusion(f32[1,2,2,3,32,32,32]{5,2,4,1,6,3,0:T(2,128)} %copy.70, pred[2,2]{1,0:T(4,128)(4,1)S(1)} %compare_and_fusion, pred[2,2]{1,0:T(4,128)(4,1)S(1)} %and.182), kind=kLoop, calls=%fused_computation.2 | loop fusion | flops 786432 | bytes 3145736 | tf_op jit(solution)/shard_map/transpose | solution.py:40
  301.5 9.5 reshape.253
  311.1 13.6 %collective-permute-start.2 = (f32[3,1,4096]{2,1,0:T(1,128)S(1)}, f32[3,1,4096]{2,1,0:T(1,128)S(1)}, u32[]{:S(2)}, u32[]{:S(2)}) collective-permute-start(f32[3,1,4096]{2,1,0:T(1,128)S(1)} %get-tuple-element.30), channel_id=1, source_target_pairs={{0,1},{1,2},{2,3},{3,4},{4,5},{5,6},{6,7},{7,8},{8,9},{9,10},{10,1... | collective-permute-start | bytes 147464 | tf_op jit(solution)/shard_map/ppermute | solution.py:27
  331.9 7.9 collective-permute-start.8
  343.8 7.9 collective-permute-start.4
  354.4 6.9 collective-permute-done.5
  382.6 154.0 %reshape.256 = f32[3,16,2,32,2,32,2]{6,5,4,3,2,1,0:T(8,128)} reshape(f32[3,32,4096]{2,1,0:T(8,128)} %fusion.34) | data formatting | bytes 3145728 | tf_op jit(solution)/shard_map/reshape | solution.py:104
  536.6 31.6 %reduce_sum.54 = f32[3,16,32,32]{3,2,1,0:T(8,128)} reduce(f32[3,16,2,32,2,32,2]{6,5,4,3,2,1,0:T(8,128)} %reshape.256, f32[]{:T(128)} %constant.250.clone.1), dimensions={2,4,6}, to_apply=%region_0.1 | reduce | flops 344064 | bytes 1769476 | tf_op jit(solution)/shard_map/reduce_sum | solution.py:105
  575.3 7.9 collective-permute-start.12
  606.6 14.7 %reshape.257 = f32[3,8,2,16,2,16,2]{6,5,4,3,2,1,0:T(8,128)} reshape(f32[3,16,1024]{2,1,0:T(8,128)} %fusion.105) | data formatting | bytes 393216 | tf_op jit(solution)/shard_map/reshape | solution.py:104
  621.3 6.3 reduce_sum.56
  644.3 7.4 collective-permute-start.22
  654.1 6.7 collective-permute-done.23
  665.4 15.4 %all_gather.7 = f32[4,64,64]{2,0,1:T(4,128)S(1)} all-gather(f32[4,4,64]{2,0,1:T(4,128)S(1)} %copy.75), channel_id=1, replica_groups=mesh['grp'=8,'dev'=16] {'dev'}, dimensions={1}, use_global_device_ids=true | all-gather | bytes 69632 | tf_op jit(solution)/shard_map/all_gather | solution.py:126
  680.8 6.6 collective-permute-start.24
  758.3 7.2 collective-permute-done.43
  783.5 10.4 reshape.260
  821.7 32.2 %broadcast_in_dim.362 = f32[3,16,2,32,2,32,2]{6,5,4,3,2,1,0:T(8,128)} broadcast(f32[3,16,32,32]{3,2,1,0:T(8,128)} %broadcast_in_dim.361), dimensions={0,1,3,5} | broadcast | bytes 1769472 | tf_op jit(solution)/shard_map/broadcast_in_dim | solution.py:112
  853.9 138.6 %reshape.261 = f32[3,32,4096]{2,1,0:T(8,128)} reshape(f32[3,16,2,32,2,32,2]{6,5,4,3,2,1,0:T(8,128)} %broadcast_in_dim.362) | data formatting | bytes 3145728 | tf_op jit(solution)/shard_map/reshape | solution.py:113
  1000.1 6.3 collective-permute-done.51
  1014.1 6.0 collective-permute-done.53
  1023.0 7.7 reshape.262
  1030.7 10.0 copy.77
  (348 shorter events, 276.4 us)
Async XLA Ops:
  6.5 260.3 %all-gather.2.cloned.1.call-start = ((), (), s32[]{:S(2)}) async-start(), calls=%async_computation.1 | async-start | bytes 26738688 | tf_op jit(solution)/shard_map/all_gather | solution.py:177
  12.0 135.1 %all-to-all-start = ((f32[16,4,32,1024]{3,2,1,0:T(8,128)}), f32[16,4,32,1024]{3,2,1,0:T(8,128)}, u32[]{:S(2)}, u32[]{:S(2)}) async-start(f32[16,4,32,1024]{3,2,1,0:T(8,128)} %stack.2), calls=%async_computation | async-start | bytes 16777216 | tf_op jit(solution)/shard_map/all_to_all | solution.py:12
  19.1 552.8 %collective-permute-start.10 = (f32[3,1,1024]{2,1,0:T(1,128)}, f32[3,1,1024]{2,1,0:T(1,128)}, u32[]{:S(2)}, u32[]{:S(2)}) collective-permute-start(f32[3,1,1024]{2,1,0:T(1,128)} %broadcast.447), channel_id=1, source_target_pairs={{0,1},{1,2},{2,3},{3,4},{4,5},{5,6},{6,7},{7,8},{8,9},{9,10},{10,1... | collective-permute-start | bytes 36872 | tf_op jit(solution)/shard_map/ppermute | solution.py:27
  23.3 550.6 %collective-permute-start.11 = (f32[3,1,1024]{2,1,0:T(1,128)}, f32[3,1,1024]{2,1,0:T(1,128)}, u32[]{:S(2)}, u32[]{:S(2)}) collective-permute-start(f32[3,1,1024]{2,1,0:T(1,128)} %broadcast.447), channel_id=1, source_target_pairs={{1,0},{2,1},{3,2},{4,3},{5,4},{6,5},{7,6},{8,7},{9,8},{10,9},{11,1... | collective-permute-start | bytes 36872 | tf_op jit(solution)/shard_map/ppermute | solution.py:29
  25.9 604.4 %collective-permute-start.18 = (f32[3,1,256]{2,1,0:T(1,128)}, f32[3,1,256]{2,1,0:T(1,128)}, u32[]{:S(2)}, u32[]{:S(2)}) collective-permute-start(f32[3,1,256]{2,1,0:T(1,128)} %broadcast.451), channel_id=1, source_target_pairs={{0,1},{1,2},{2,3},{3,4},{4,5},{5,6},{6,7},{7,8},{8,9},{9,10},{10,1... | collective-permute-start | bytes 9224 | tf_op jit(solution)/shard_map/ppermute | solution.py:27
  205.8 105.3 %collective-permute-start = (f32[1,1,4096]{2,1,0:T(1,128)S(1)}, f32[1,1,4096]{2,1,0:T(1,128)S(1)}, u32[]{:S(2)}, u32[]{:S(2)}) collective-permute-start(f32[1,1,4096]{2,1,0:T(1,128)S(1)} %get-tuple-element.39), channel_id=1, source_target_pairs={{0,1},{1,2},{2,3},{3,4},{4,5},{5,6},{6,7},{7,8},{8,9},{9,10},{10,1... | collective-permute-start | bytes 49160 | tf_op jit(solution)/shard_map/ppermute | solution.py:27
  250.9 73.8 %collective-permute-start.1 = (f32[1,1,4096]{2,1,0:T(1,128)S(1)}, f32[1,1,4096]{2,1,0:T(1,128)S(1)}, u32[]{:S(2)}, u32[]{:S(2)}) collective-permute-start(f32[1,1,4096]{2,1,0:T(1,128)S(1)} %get-tuple-element.40), channel_id=1, source_target_pairs={{1,0},{2,1},{3,2},{4,3},{5,4},{6,5},{7,6},{8,7},{9,8},{10,9},{11,1... | collective-permute-start | bytes 49160 | tf_op jit(solution)/shard_map/ppermute | solution.py:29
  311.1 20.8 %collective-permute-start.2 = (f32[3,1,4096]{2,1,0:T(1,128)S(1)}, f32[3,1,4096]{2,1,0:T(1,128)S(1)}, u32[]{:S(2)}, u32[]{:S(2)}) collective-permute-start(f32[3,1,4096]{2,1,0:T(1,128)S(1)} %get-tuple-element.30), channel_id=1, source_target_pairs={{0,1},{1,2},{2,3},{3,4},{4,5},{5,6},{6,7},{7,8},{8,9},{9,10},{10,1... | collective-permute-start | bytes 147464 | tf_op jit(solution)/shard_map/ppermute | solution.py:27
  324.7 15.0 %collective-permute-start.3 = (f32[3,1,4096]{2,1,0:T(1,128)S(1)}, f32[3,1,4096]{2,1,0:T(1,128)S(1)}, u32[]{:S(2)}, u32[]{:S(2)}) collective-permute-start(f32[3,1,4096]{2,1,0:T(1,128)S(1)} %get-tuple-element.31), channel_id=1, source_target_pairs={{1,0},{2,1},{3,2},{4,3},{5,4},{6,5},{7,6},{8,7},{9,8},{10,9},{11,1... | collective-permute-start | bytes 147464 | tf_op jit(solution)/shard_map/ppermute | solution.py:29
  331.9 11.9 %collective-permute-start.8 = (f32[1,1,1024]{2,1,0:T(1,128)S(1)}, f32[1,1,1024]{2,1,0:T(1,128)S(1)}, u32[]{:S(2)}, u32[]{:S(2)}) collective-permute-start(f32[1,1,1024]{2,1,0:T(1,128)S(1)} %get-tuple-element.73), channel_id=1, source_target_pairs={{0,1},{1,2},{2,3},{3,4},{4,5},{5,6},{6,7},{7,8},{8,9},{9,10},{10,1... | collective-permute-start | bytes 12296 | tf_op jit(solution)/shard_map/ppermute | solution.py:27
  339.8 11.9 %collective-permute-start.9 = (f32[1,1,1024]{2,1,0:T(1,128)S(1)}, f32[1,1,1024]{2,1,0:T(1,128)S(1)}, u32[]{:S(2)}, u32[]{:S(2)}) collective-permute-start(f32[1,1,1024]{2,1,0:T(1,128)S(1)} %get-tuple-element.74), channel_id=1, source_target_pairs={{1,0},{2,1},{3,2},{4,3},{5,4},{6,5},{7,6},{8,7},{9,8},{10,9},{11,1... | collective-permute-start | bytes 12296 | tf_op jit(solution)/shard_map/ppermute | solution.py:29
  343.8 10.6 %collective-permute-start.4 = (f32[3,1,4096]{2,1,0:T(1,128)S(1)}, f32[3,1,4096]{2,1,0:T(1,128)S(1)}, u32[]{:S(2)}, u32[]{:S(2)}) collective-permute-start(f32[3,1,4096]{2,1,0:T(1,128)S(1)} %get-tuple-element.28), channel_id=1, source_target_pairs={{0,1},{1,2},{2,3},{3,4},{4,5},{5,6},{6,7},{7,8},{8,9},{9,10},{10,1... | collective-permute-start | bytes 147464 | tf_op jit(solution)/shard_map/ppermute | solution.py:27
  351.7 9.6 collective-permute-start.5
  365.4 9.6 collective-permute-start.7
  369.5 260.8 %collective-permute-start.19 = (f32[3,1,256]{2,1,0:T(1,128)}, f32[3,1,256]{2,1,0:T(1,128)}, u32[]{:S(2)}, u32[]{:S(2)}) collective-permute-start(f32[3,1,256]{2,1,0:T(1,128)} %broadcast.451), channel_id=1, source_target_pairs={{1,0},{2,1},{3,2},{4,3},{5,4},{6,5},{7,6},{8,7},{9,8},{10,9},{11,1... | collective-permute-start | bytes 9224 | tf_op jit(solution)/shard_map/ppermute | solution.py:29
  375.0 208.2 %collective-permute-start.16 = (f32[1,1,256]{2,1,0:T(1,128)}, f32[1,1,256]{2,1,0:T(1,128)}, u32[]{:S(2)}, u32[]{:S(2)}) collective-permute-start(f32[1,1,256]{2,1,0:T(1,128)} %get-tuple-element.89), channel_id=1, source_target_pairs={{0,1},{1,2},{2,3},{3,4},{4,5},{5,6},{6,7},{7,8},{8,9},{9,10},{10,1... | collective-permute-start | bytes 3080 | tf_op jit(solution)/shard_map/ppermute | solution.py:27
  571.9 13.2 %collective-permute-start.17 = (f32[1,1,256]{2,1,0:T(1,128)}, f32[1,1,256]{2,1,0:T(1,128)S(1)}, u32[]{:S(2)}, u32[]{:S(2)}) collective-permute-start(f32[1,1,256]{2,1,0:T(1,128)} %get-tuple-element.90), channel_id=1, source_target_pairs={{1,0},{2,1},{3,2},{4,3},{5,4},{6,5},{7,6},{8,7},{9,8},{10,9},{11,1... | collective-permute-start | bytes 3080 | tf_op jit(solution)/shard_map/ppermute | solution.py:29
  575.3 11.2 %collective-permute-start.12 = (f32[3,1,1024]{2,1,0:T(1,128)S(1)}, f32[3,1,1024]{2,1,0:T(1,128)S(1)}, u32[]{:S(2)}, u32[]{:S(2)}) collective-permute-start(f32[3,1,1024]{2,1,0:T(1,128)S(1)} %get-tuple-element.47), channel_id=1, source_target_pairs={{0,1},{1,2},{2,3},{3,4},{4,5},{5,6},{6,7},{7,8},{8,9},{9,10},{10,1... | collective-permute-start | bytes 36872 | tf_op jit(solution)/shard_map/ppermute | solution.py:27
  583.2 9.2 collective-permute-start.13
  595.7 9.2 collective-permute-start.15
  631.2 12.9 %collective-permute-start.20 = (f32[3,1,256]{2,1,0:T(1,128)S(1)}, f32[3,1,256]{2,1,0:T(1,128)S(1)}, u32[]{:S(2)}, u32[]{:S(2)}) collective-permute-start(f32[3,1,256]{2,1,0:T(1,128)S(1)} %get-tuple-element.81), channel_id=1, source_target_pairs={{0,1},{1,2},{2,3},{3,4},{4,5},{5,6},{6,7},{7,8},{8,9},{9,10},{10,1... | collective-permute-start | bytes 9224 | tf_op jit(solution)/shard_map/ppermute | solution.py:27
  633.4 10.7 %collective-permute-start.21 = (f32[3,1,256]{2,1,0:T(1,128)S(1)}, f32[3,1,256]{2,1,0:T(1,128)S(1)}, u32[]{:S(2)}, u32[]{:S(2)}) collective-permute-start(f32[3,1,256]{2,1,0:T(1,128)S(1)} %get-tuple-element.82), channel_id=1, source_target_pairs={{1,0},{2,1},{3,2},{4,3},{5,4},{6,5},{7,6},{8,7},{9,8},{10,9},{11,1... | collective-permute-start | bytes 9224 | tf_op jit(solution)/shard_map/ppermute | solution.py:29
  637.1 55.6 %collective-permute-start.26 = (f32[3,1,64]{2,0,1:T(4,128)}, f32[3,1,64]{2,0,1:T(4,128)}, u32[]{:S(2)}, u32[]{:S(2)}) collective-permute-start(f32[3,1,64]{2,0,1:T(4,128)} %broadcast.455), channel_id=1, source_target_pairs={{0,16},{16,32},{32,48},{48,64},{64,80},{80,96},{96,112},{1,17},{17... | collective-permute-start | bytes 2312 | tf_op jit(solution)/shard_map/ppermute | solution.py:27
  639.0 53.7 %collective-permute-start.27 = (f32[3,1,64]{2,0,1:T(4,128)}, f32[3,1,64]{2,0,1:T(4,128)}, u32[]{:S(2)}, u32[]{:S(2)}) collective-permute-start(f32[3,1,64]{2,0,1:T(4,128)} %broadcast.455), channel_id=1, source_target_pairs={{16,0},{32,16},{48,32},{64,48},{80,64},{96,80},{112,96},{17,1},{33... | collective-permute-start | bytes 2312 | tf_op jit(solution)/shard_map/ppermute | solution.py:29
  644.3 9.9 collective-permute-start.22
  651.7 9.1 collective-permute-start.23
  756.4 9.1 collective-permute-start.43
  767.7 9.1 collective-permute-start.45
  796.9 9.2 collective-permute-start.47
  809.4 9.2 collective-permute-start.49
  996.7 9.6 collective-permute-start.51
  1010.5 9.6 collective-permute-start.53
  (91 other events, 4279.3 us)
Sparse Core Ops, SparseCore 0:
  9.6 257.2 all-gather.1
